TPU v7x, 32 devices: a whole 2x2x4 slice. The times are simulated.
32 devices in a mesh: dp: 4 (over z), ctx: 8 (over y, x, core).
Axes of the slice: x: 2, y: 2, z: 4, core: 2. Of those that a mesh axis runs over, the one named last changes fastest.
Arguments:
- queries: bfloat16 [4, 1024, 6144], P('dp', 'ctx'), may hold values from -6 to 6
- kv_proj: bfloat16 [4, 3072, 1024], P('dp', 'ctx'), may hold values from -6 to 6
- hidden: bfloat16 [4, 3072, 12288], P('dp', 'ctx'), may hold values from -0.119628906 to 0.119628906
- grad_out: bfloat16 [4, 1024, 6144], P('dp', 'ctx'), may hold values from -6 to 6
- doc_lengths: int32 [4, 256], P('dp'), may hold values from 1 to 8192, 262144 in all within a row
- slab_offsets: int32 [4], P('dp'), may hold values from 0 to 261120
Outputs:
- attended: bfloat16 [4, 1024, 6144], P('dp', 'ctx')
- grad_queries: bfloat16 [4, 1024, 6144], P('dp', 'ctx')
- grad_kv: bfloat16 [4, 3072, 1024], P('dp', 'ctx')
- grad_weight: float32 [12288, 1024], P('ctx', 'dp')
All inputs are finite; a program needn't handle non-finite values.
Results may differ from a plain program's by a relative error of at most 0.025.
Values may be sent and summed in bfloat16 or wider, within the bound.
A program may use at most 192 MiB of HBM per device.

v0:
```python
import functools

import jax
import jax.numpy as jnp
from jax import lax
from jax.experimental import pallas as pl
from jax.experimental.pallas import tpu as pltpu
from jax.sharding import PartitionSpec as P

HD = 128
KV_HEADS = 4
WINDOW = 2048
BLK = 256
LOG2E = 1.4426950408889634
FACTOR = HD ** (-0.5)
NT = (((1,), (1,)), ((), ()))
NN = (((1,), (0,)), ((), ()))


def dot(a, b, dims=NN):
    return lax.dot_general(a, b, dims, preferred_element_type=jnp.float32)


def attention_kernel(
    heads, n, low_ref, q_hbm, go_hbm, kv_hbm, hid_hbm,
    att_hbm, gq_hbm, hid_out, grads_ref,
    q_all, go_all, kv_all, att_all, gq_all,
    scores, kt, vt, qs, gs, wlow, dlow, mx, tot, acc, delta,
    send, recv, own, out_send, out_recv, out_own,
):
    f32, bf16 = jnp.float32, jnp.bfloat16
    me = lax.axis_index("ctx")
    rows, kb = q_hbm.shape[0], kv_hbm.shape[0]
    width, feats = heads * HD, hid_out.shape[2]
    repeat = n // KV_HEADS
    chunks = kt.shape[0]
    span = scores.shape[0]
    per = BLK // rows

    def mod(k):
        return lax.rem(me + k, n)

    barrier = pltpu.get_barrier_semaphore()
    for k in range(1, n):
        pl.semaphore_signal(
            barrier, inc=1, device_id={"ctx": mod(k)}, device_id_type=pl.DeviceIdType.MESH
        )
    pl.semaphore_wait(barrier, n - 1)

    def ends(a, dest, source):
        if a == 0:
            cols = pl.ds(pl.multiple_of((dest // repeat) * (2 * HD), 2 * HD), 2 * HD)
            return kv_hbm.at[:, cols], kv_all.at[pl.ds(pl.multiple_of(source * kb, kb), kb)]
        if a == 3:
            cols = pl.ds(pl.multiple_of(dest * feats, feats), feats)
            return hid_hbm.at[:, cols], hid_out.at[source]
        cols = pl.ds(pl.multiple_of(dest * width, width), width)
        where = pl.ds(pl.multiple_of(source * rows, rows), rows)
        src, dst = ((q_hbm, q_all), (go_hbm, go_all))[a - 1]
        return src.at[:, cols], dst.at[where]

    def remote(a, dest, source):
        src, dst = ends(a, dest, source)
        return pltpu.make_async_remote_copy(
            src_ref=src,
            dst_ref=dst,
            send_sem=send.at[a, dest],
            recv_sem=recv.at[a, source],
            device_id={"ctx": dest},
            device_id_type=pl.DeviceIdType.MESH,
        )

    def here(a):
        src, dst = ends(a, me, me)
        return pltpu.make_async_copy(src, dst, own.at[a])

    for a in range(4):
        for k in range(1, n):
            remote(a, mod(k), me).start()
        here(a).start()

    grads_ref[...] = jnp.zeros_like(grads_ref)
    lane = lax.broadcasted_iota(jnp.int32, (BLK, BLK), 1)
    sub = lax.broadcasted_iota(jnp.int32, (BLK, BLK), 0)

    for a in range(3):
        here(a).wait()
        for k in range(1, n):
            remote(a, me, mod(k)).wait_recv()

    def prep(c, carry):
        keys = pl.ds(pl.multiple_of(c * BLK, BLK), BLK)
        kt[c] = kv_all[keys, :HD].astype(f32).T.astype(bf16)
        vt[c] = kv_all[keys, HD:].astype(f32).T.astype(bf16)
        return carry

    lax.fori_loop(0, chunks, prep, 0)

    def out_ends(which, dest, source):
        cols = pl.ds(pl.multiple_of(source * width, width), width)
        where = pl.ds(pl.multiple_of(dest * rows, rows), rows)
        src, dst = ((att_all, att_hbm), (gq_all, gq_hbm))[which]
        return src.at[where], dst.at[:, cols]

    def out_remote(which, dest, source):
        src, dst = out_ends(which, dest, source)
        return pltpu.make_async_remote_copy(
            src_ref=src,
            dst_ref=dst,
            send_sem=out_send.at[which, dest],
            recv_sem=out_recv.at[which, source],
            device_id={"ctx": dest},
            device_id_type=pl.DeviceIdType.MESH,
        )

    def out_here(which):
        src, dst = out_ends(which, me, me)
        return pltpu.make_async_copy(src, dst, out_own.at[which])

    def block(qb, carry):
        mine = pl.ds(pl.multiple_of(qb * BLK, BLK), BLK)
        for h in range(heads):
            qs[h * BLK : (h + 1) * BLK] = q_all[mine, h * HD : (h + 1) * HD]
            gs[h * BLK : (h + 1) * BLK] = go_all[mine, h * HD : (h + 1) * HD]
        mx[...] = jnp.full(mx.shape, -1e30, f32)
        tot[...] = jnp.zeros(tot.shape, f32)
        acc[...] = jnp.zeros(acc.shape, f32)
        low = low_ref[qb]

        def score_step(t, carry):
            c = qb + t
            keys = pl.ds(pl.multiple_of(c * BLK, BLK), BLK)
            key = kv_all[keys, :HD]
            j = sub + c * BLK
            ok = (j >= low) & (j <= lane + (qb * BLK + WINDOW))
            for h in range(heads):
                cols = slice(h * BLK, (h + 1) * BLK)
                s = dot(key, qs[cols, :], NT)
                s = jnp.where(ok, s, -1e30)
                scores[t, :, cols] = s
                part = jnp.max(s.reshape(BLK // 8, 8, BLK), axis=0)
                mx[:, cols] = jnp.maximum(mx[:, cols], part)
            return carry

        lax.fori_loop(0, span, score_step, 0)
        mx[0:1, :] = jnp.max(mx[...], axis=0, keepdims=True) * (FACTOR * LOG2E)

        def value_step(t, carry):
            for h in range(heads):
                cols = slice(h * BLK, (h + 1) * BLK)
                p = jnp.exp2(scores[t, :, cols] * (FACTOR * LOG2E) - mx[0:1, cols])
                scores[t, :, cols] = p
                tot[:, cols] += jnp.sum(p.reshape(BLK // 8, 8, BLK), axis=0)
                acc[:, cols] += dot(vt[qb + t], p.astype(bf16))
            return carry

        lax.fori_loop(0, span, value_step, 0)
        tot[0:1, :] = 1.0 / jnp.sum(tot[...], axis=0, keepdims=True)
        for h in range(heads):
            cols = slice(h * BLK, (h + 1) * BLK)
            att = (acc[:, cols] * tot[0:1, cols]).T.astype(bf16)
            att_all[mine, h * HD : (h + 1) * HD] = att
            prod = att.astype(f32) * gs[cols, :].astype(f32)
            delta[0:1, cols] = jnp.sum(prod.T, axis=0, keepdims=True)
        acc[...] = jnp.zeros(acc.shape, f32)

        def grad_step(t, carry):
            keys = pl.ds(pl.multiple_of((qb + t) * BLK, BLK), BLK)
            value = kv_all[keys, HD:]
            for h in range(heads):
                cols = slice(h * BLK, (h + 1) * BLK)
                w = scores[t, :, cols] * tot[0:1, cols]
                gp = dot(value, gs[cols, :], NT)
                ds = (w * (gp - delta[0:1, cols])).astype(bf16)
                wlow[:, cols] = w.astype(bf16)
                dlow[:, cols] = ds
                acc[:, cols] += dot(kt[qb + t], ds)
            grads_ref[keys, :HD] += dot(dlow[...], qs[...]) * FACTOR
            grads_ref[keys, HD:] += dot(wlow[...], gs[...])
            return carry

        lax.fori_loop(0, span, grad_step, 0)
        for h in range(heads):
            cols = slice(h * BLK, (h + 1) * BLK)
            gq_all[mine, h * HD : (h + 1) * HD] = (acc[:, cols] * FACTOR).T.astype(bf16)
        for u in range(per):
            dest = qb * per + u

            @pl.when(dest == me)
            def _():
                for which in range(2):
                    out_here(which).start()

            @pl.when(dest != me)
            def _():
                for which in range(2):
                    out_remote(which, dest, me).start()

        return carry

    lax.fori_loop(0, q_all.shape[0] // BLK, block, 0)

    here(3).wait()
    for which in range(2):
        out_here(which).wait()
    for k in range(1, n):
        remote(3, me, mod(k)).wait_recv()
        for which in range(2):
            out_remote(which, me, mod(k)).wait_recv()
    for k in range(1, n):
        for a in range(4):
            remote(a, mod(k), me).wait_send()
        for which in range(2):
            out_remote(which, mod(k), me).wait_send()


def attention(low, queries, grad_out, kv_proj, hidden):
    n = lax.axis_size("ctx")
    rows, total_width = queries.shape
    kb = kv_proj.shape[0]
    width, feats = total_width // n, hidden.shape[1] // n
    total, keys = rows * n, kb * n
    heads = width // HD
    f32, bf16 = jnp.float32, jnp.bfloat16
    wide = heads * BLK
    span = WINDOW // BLK + 1
    chunks = keys // BLK
    hbm = pl.BlockSpec(memory_space=pl.ANY)
    vmem = pl.BlockSpec(memory_space=pltpu.VMEM)
    dma = pltpu.SemaphoreType.DMA
    return pl.pallas_call(
        functools.partial(attention_kernel, heads, n),
        in_specs=[vmem, hbm, hbm, hbm, hbm],
        out_specs=[hbm, hbm, hbm, vmem],
        scratch_shapes=[
            pltpu.VMEM((total, width), bf16),
            pltpu.VMEM((total, width), bf16),
            pltpu.VMEM((keys, 2 * HD), bf16),
            pltpu.VMEM((total, width), bf16),
            pltpu.VMEM((total, width), bf16),
            pltpu.VMEM((span, BLK, wide), f32),
            pltpu.VMEM((chunks, HD, BLK), bf16),
            pltpu.VMEM((chunks, HD, BLK), bf16),
            pltpu.VMEM((wide, HD), bf16),
            pltpu.VMEM((wide, HD), bf16),
            pltpu.VMEM((BLK, wide), bf16),
            pltpu.VMEM((BLK, wide), bf16),
            pltpu.VMEM((8, wide), f32),
            pltpu.VMEM((8, wide), f32),
            pltpu.VMEM((HD, wide), f32),
            pltpu.VMEM((8, wide), f32),
            dma((4, n)),
            dma((4, n)),
            dma((4,)),
            dma((2, n)),
            dma((2, n)),
            dma((2,)),
        ],
        out_shape=[
            jax.ShapeDtypeStruct((rows, total_width), bf16),
            jax.ShapeDtypeStruct((rows, total_width), bf16),
            jax.ShapeDtypeStruct((n, kb, feats), bf16),
            jax.ShapeDtypeStruct((keys, 2 * HD), f32),
        ],
        compiler_params=pltpu.CompilerParams(
            collective_id=0, has_side_effects=True, vmem_limit_bytes=52 * 1024 * 1024
        ),
        cost_estimate=pl.CostEstimate(
            flops=20 * total * (WINDOW + BLK) * width,
            bytes_accessed=12 * total * width,
            transcendentals=total * (WINDOW + BLK) * heads,
        ),
        name="attention",
    )(low, queries, grad_out, kv_proj, hidden)


def weight_kernel(idx_ref, g_ref, hid_ref, out_ref):
    total = dot(g_ref[0, 0], hid_ref[0])
    for r in range(1, hid_ref.shape[0]):
        total = total + dot(g_ref[0, r], hid_ref[r])
    out_ref[...] = total.astype(out_ref.dtype)


def weight_part(idx, gathered, hidden, width, dtype):
    repeat, kr, feats = hidden.shape
    tile = 256 if feats % 512 else 512
    return pl.pallas_call(
        weight_kernel,
        grid_spec=pltpu.PrefetchScalarGridSpec(
            num_scalar_prefetch=1,
            grid=(pl.cdiv(feats, tile),),
            in_specs=[
                pl.BlockSpec((1, repeat, width, kr), lambda i, s: (s[0], 0, s[1], 0)),
                pl.BlockSpec((repeat, kr, tile), lambda i, s: (0, 0, i)),
            ],
            out_specs=pl.BlockSpec((width, tile), lambda i, s: (0, i)),
        ),
        out_shape=jax.ShapeDtypeStruct((width, feats), dtype),
        compiler_params=pltpu.CompilerParams(vmem_limit_bytes=32 * 1024 * 1024),
        cost_estimate=pl.CostEstimate(
            flops=2 * repeat * kr * feats * width,
            bytes_accessed=2 * repeat * kr * feats,
            transcendentals=0,
        ),
        name="weight",
    )(idx, gathered, hidden)


def local(queries, kv_proj, hidden, grad_out, doc_lengths, slab_offsets):
    i32, f32, bf16 = jnp.int32, jnp.float32, jnp.bfloat16
    n = lax.axis_size("ctx")
    dp = lax.axis_size("dp")
    me = lax.axis_index("ctx")
    my_dp = lax.axis_index("dp")
    repeat = n // KV_HEADS
    rows = queries.shape[1]
    kb, kv_width = kv_proj.shape[1:]
    total_rows = rows * n
    keys = kb * n

    bounds = jnp.cumsum(doc_lengths[0], dtype=i32)
    offset = slab_offsets[0]
    index = jnp.arange(total_rows, dtype=i32)
    pos = offset + index
    start = jnp.max(jnp.where(bounds[None, :] <= pos[:, None], bounds[None, :], 0), axis=1)
    low = jnp.maximum(index + 1, jnp.maximum(start, 0) - offset + WINDOW)
    low = low.reshape(total_rows // BLK, 1, BLK)
    attended, grad_query, hid, grads = attention(
        low, queries[0], grad_out[0], kv_proj[0], hidden[0]
    )
    kr = keys // repeat
    hid = hid.reshape(repeat, kr, hid.shape[2])

    parts = grads.reshape(repeat, keys // repeat, 2 * HD)
    rank = me % repeat
    mine = lax.dynamic_index_in_dim(parts, rank, 0, keepdims=False)
    for k in range(1, repeat):
        sent = lax.dynamic_index_in_dim(parts, rank ^ k, 0, keepdims=False)
        mine = mine + lax.ppermute(sent, "ctx", [(i, i ^ k) for i in range(n)])
    gathered = lax.all_gather(mine.astype(bf16).T, "ctx", axis=0)
    gathered = gathered.reshape(KV_HEADS, repeat, 2 * HD, kr)
    mine_low = lax.dynamic_index_in_dim(gathered, me * kb // kr, 1, keepdims=False)
    mine_low = lax.dynamic_slice_in_dim(mine_low, me * kb % kr, kb, 2)
    grad_low = mine_low.transpose(2, 0, 1).reshape(kb, kv_width)

    cols = kv_width // dp
    per = 2 * HD // cols

    def part(k, dtype):
        t = (my_dp ^ k).astype(i32)
        return weight_part(jnp.stack([t // per, t % per]), gathered, hid, cols, dtype)

    sent = []
    for k in sorted(range(1, dp), key=lambda k: (k != 2, k)):
        sent.append(lax.ppermute(part(k, bf16), "dp", [(i, i ^ k) for i in range(dp)]))
    weight = part(0, f32)

    for s in sent:
        weight = weight + s.astype(f32)
    return (attended[None], grad_query[None], grad_low[None], weight.T)


def solution(mesh):
    in_specs = (
        P("dp", "ctx", None),
        P("dp", "ctx", None),
        P("dp", "ctx", None),
        P("dp", "ctx", None),
        P("dp", None),
        P("dp"),
    )
    out_specs = (P("dp", "ctx", None), P("dp", "ctx", None), P("dp", "ctx", None), P("ctx", "dp"))
    return jax.shard_map(local, mesh=mesh, in_specs=in_specs, out_specs=out_specs, check_vma=False)
```

profile of v0, /device:TPU:17, one launch (start us, length us, event | category | flops | bytes accessed | tf_op | source)
XLA Modules:
  0.0 355.3 jit_solution(967371315931815810)
XLA Ops:
  10.7 192.1 %attention.1 = (bf16[128,6144]{1,0:T(8,128)(2,1)}, bf16[128,6144]{1,0:T(8,128)(2,1)}, bf16[8,384,1536]{2,1,0:T(8,128)(2,1)}, f32[3072,256]{1,0:T(8,128)}) custom-call(s32[4,1,256]{2,1,0:T(1,128)S(1)} %add_maximum_fusion.low_ref, bf16[128,6144]{1,0:T(8,128)(2,1)} %bitcast.54, bf16[128,6144]{1,0:T(8,128)(2,1)} %bitcast.55, bf16[384,1024]{1,0:T(8,128)(2,1)S(1)} %bitcast.45, ...), custom_call_target="tpu_custom_call" | custom-call | flops 36238786560 | bytes 9437184 | tf_op jit(solution)/shard_map/attention/pallas_call | solution.py:231
  202.8 2.1 constant_dynamic-slice_fusion.2
  204.9 1.6 copy.18
  207.0 3.3 collective-permute-done
  210.3 2.5 fusion.1
  212.9 47.0 %all-gather.3.cloned.1.call-done = bf16[2048,1536]{1,0:T(8,128)(2,1)} async-done(((bf16[256,1536]{1,0:T(8,128)(2,1)}), bf16[2048,1536]{1,0:T(8,128)(2,1)}) %all-gather.3.cloned.1.call-update) | async-done | bytes 6291472 | tf_op jit(solution)/shard_map/all_gather | solution.py:340
  259.9 3.7 %copy-done = bf16[8,384,1536]{2,1,0:T(8,128)(2,1)S(1)} copy-done((bf16[8,384,1536]{2,1,0:T(8,128)(2,1)S(1)}, bf16[8,384,1536]{2,1,0:T(8,128)(2,1)}, u32[]{:S(2)}) %copy-start) | copy-done | bytes 9437208
  263.6 2.8 copy-done.2
  266.4 4.2 %weight.5 = bf16[256,1536]{1,0:T(8,128)(2,1)S(1)} custom-call(s32[2]{0:T(128)S(1)} %pad_add_fusion.2.idx_ref, bf16[4,2,256,1536]{3,2,1,0:T(8,128)(2,1)S(1)} %bitcast.41, bf16[2,1536,1536]{2,1,0:T(8,128)(2,1)S(1)} %bitcast.36), custom_call_target="tpu_custom_call" | custom-call | flops 2415919104 | bytes 9437184 | tf_op jit(solution)/shard_map/weight/pallas_call | solution.py:287
  270.9 4.2 %weight.6 = bf16[256,1536]{1,0:T(8,128)(2,1)S(1)} custom-call(s32[2]{0:T(128)S(1)} %get-tuple-element.27.idx_ref, bf16[4,2,256,1536]{3,2,1,0:T(8,128)(2,1)S(1)} %bitcast.42, bf16[2,1536,1536]{2,1,0:T(8,128)(2,1)S(1)} %bitcast.37), custom_call_target="tpu_custom_call" | custom-call | flops 2415919104 | bytes 9437184 | tf_op jit(solution)/shard_map/weight/pallas_call | solution.py:287
  275.0 1.3 collective-permute-start.2
  276.3 4.2 %weight.7 = bf16[256,1536]{1,0:T(8,128)(2,1)S(1)} custom-call(s32[2]{0:T(128)S(1)} %get-tuple-element.26.idx_ref, bf16[4,2,256,1536]{3,2,1,0:T(8,128)(2,1)S(1)} %bitcast.43, bf16[2,1536,1536]{2,1,0:T(8,128)(2,1)S(1)} %bitcast.38), custom_call_target="tpu_custom_call" | custom-call | flops 2415919104 | bytes 9437184 | tf_op jit(solution)/shard_map/weight/pallas_call | solution.py:287
  280.5 1.3 collective-permute-start.3
  281.8 1.6 constant_dynamic-slice_fusion
  283.4 1.2 copy.19
  284.6 3.7 %copy-done.1 = bf16[8,384,1536]{2,1,0:T(8,128)(2,1)S(1)} copy-done((bf16[8,384,1536]{2,1,0:T(8,128)(2,1)S(1)}, bf16[8,384,1536]{2,1,0:T(8,128)(2,1)}, u32[]{:S(2)}) %copy-start.1) | copy-done | bytes 9437208
  288.3 2.8 copy-done.3
  291.0 4.2 %weight.4 = f32[256,1536]{1,0:T(8,128)S(1)} custom-call(s32[2]{0:T(128)S(1)} %pad_add_fusion.3.idx_ref, bf16[4,2,256,1536]{3,2,1,0:T(8,128)(2,1)S(1)} %bitcast.44, bf16[2,1536,1536]{2,1,0:T(8,128)(2,1)S(1)} %bitcast.39), custom_call_target="tpu_custom_call" | custom-call | flops 2415919104 | bytes 9437184 | tf_op jit(solution)/shard_map/weight/pallas_call | solution.py:287
  295.3 9.2 %collective-permute-done.1 = bf16[256,1536]{1,0:T(8,128)(2,1)} collective-permute-done((bf16[256,1536]{1,0:T(8,128)(2,1)S(1)}, bf16[256,1536]{1,0:T(8,128)(2,1)}, u32[]{:S(2)}, u32[]{:S(2)}) %collective-permute-start.1) | collective-permute-done | bytes 786464 | tf_op jit(solution)/shard_map/ppermute | solution.py:355
  304.5 21.8 %collective-permute-done.2 = bf16[256,1536]{1,0:T(8,128)(2,1)} collective-permute-done((bf16[256,1536]{1,0:T(8,128)(2,1)S(1)}, bf16[256,1536]{1,0:T(8,128)(2,1)}, u32[]{:S(2)}, u32[]{:S(2)}) %collective-permute-start.2) | collective-permute-done | bytes 786464 | tf_op jit(solution)/shard_map/ppermute | solution.py:355
  326.3 15.5 %collective-permute-done.3 = bf16[256,1536]{1,0:T(8,128)(2,1)} collective-permute-done((bf16[256,1536]{1,0:T(8,128)(2,1)S(1)}, bf16[256,1536]{1,0:T(8,128)(2,1)}, u32[]{:S(2)}, u32[]{:S(2)}) %collective-permute-start.3) | collective-permute-done | bytes 786464 | tf_op jit(solution)/shard_map/ppermute | solution.py:355
  341.7 2.0 add_bitcast_fusion
  343.7 1.6 copy.20
  345.3 1.1 copy.24
  (28 shorter events, 5.8 us)
Async XLA Ops:
  7.2 252.8 %all-gather.3.cloned.1.call-start = ((), (), s32[]{:S(2)}) async-start(), calls=%async_computation | async-start | bytes 7077888 | tf_op jit(solution)/shard_map/all_gather | solution.py:340
  9.6 1.1 copy-start.4
  206.5 3.8 %collective-permute-start = (f32[1536,256]{0,1:T(8,128)}, f32[1536,256]{0,1:T(8,128)}, u32[]{:S(2)}, u32[]{:S(2)}) collective-permute-start(f32[1536,256]{0,1:T(8,128)} %bitcast.50), channel_id=1, source_target_pairs={{0,1},{1,0},{2,3},{3,2},{4,5},{5,4},{6,7},{7,6},{8,9},{9,8},{10,11... | collective-permute-start | bytes 4718600 | tf_op jit(solution)/shard_map/ppermute | solution.py:339
  259.9 3.7 %copy-start = (bf16[8,384,1536]{2,1,0:T(8,128)(2,1)S(1)}, bf16[8,384,1536]{2,1,0:T(8,128)(2,1)}, u32[]{:S(2)}) copy-start(bf16[8,384,1536]{2,1,0:T(8,128)(2,1)} %get-tuple-element.11) | copy-start | bytes 28311556
  263.6 2.8 copy-start.2
  270.6 33.9 %collective-permute-start.1 = (bf16[256,1536]{1,0:T(8,128)(2,1)S(1)}, bf16[256,1536]{1,0:T(8,128)(2,1)}, u32[]{:S(2)}, u32[]{:S(2)}) collective-permute-start(bf16[256,1536]{1,0:T(8,128)(2,1)S(1)} %weight.5), channel_id=1, source_target_pairs={{0,16},{8,24},{16,0},{24,8},{1,17},{9,25},{17,1},{25,9},{2,18},{10... | collective-permute-start | bytes 2359304 | tf_op jit(solution)/shard_map/ppermute | solution.py:355
  275.0 51.3 %collective-permute-start.2 = (bf16[256,1536]{1,0:T(8,128)(2,1)S(1)}, bf16[256,1536]{1,0:T(8,128)(2,1)}, u32[]{:S(2)}, u32[]{:S(2)}) collective-permute-start(bf16[256,1536]{1,0:T(8,128)(2,1)S(1)} %weight.6), channel_id=1, source_target_pairs={{0,8},{8,0},{16,24},{24,16},{1,9},{9,1},{17,25},{25,17},{2,10},{10... | collective-permute-start | bytes 2359304 | tf_op jit(solution)/shard_map/ppermute | solution.py:355
  280.5 61.3 %collective-permute-start.3 = (bf16[256,1536]{1,0:T(8,128)(2,1)S(1)}, bf16[256,1536]{1,0:T(8,128)(2,1)}, u32[]{:S(2)}, u32[]{:S(2)}) collective-permute-start(bf16[256,1536]{1,0:T(8,128)(2,1)S(1)} %weight.7), channel_id=1, source_target_pairs={{0,24},{8,16},{16,8},{24,0},{1,25},{9,17},{17,9},{25,1},{2,26},{10... | collective-permute-start | bytes 2359304 | tf_op jit(solution)/shard_map/ppermute | solution.py:355
  284.6 3.7 %copy-start.1 = (bf16[8,384,1536]{2,1,0:T(8,128)(2,1)S(1)}, bf16[8,384,1536]{2,1,0:T(8,128)(2,1)}, u32[]{:S(2)}) copy-start(bf16[8,384,1536]{2,1,0:T(8,128)(2,1)} %get-tuple-element.11) | copy-start | bytes 28311556
  288.3 2.8 copy-start.3
  343.7 1.6 copy-start.6
  345.3 2.0 copy-start.5
Sparse Core Ops, SparseCore 0:
  212.9 46.9 all-gather.2
where the time goes:
time: 356 us; the launch traced here: 355 us
  Pallas kernels  209 us (59%)
  waiting for transfers between devices  96.7 us (27%)
  local copies, waits for them, and re-layouts  25.9 us (7%)
  between operations  14.8 us (4%)
  other arithmetic  6.14 us (2%)
    pallas_call x1, Pallas kernels, attention(): pl.pallas_call(functools.partial(attention_kernel, heads, n), in_specs=[v...  192 us
    all_gather x1, waiting for transfers between devices, local(): gathered = lax.all_gather(mine.astype(bf16).T, 'ctx', axis=0)  47 us
    ppermute x3, waiting for transfers between devices, local(): lax.ppermute(part(k, bf16), 'dp', [(i, i ^ k) for i in range(dp)])  46.4 us
    unnamed x18, local copies, waits for them, and re-layouts  20 us
    pallas_call x4, Pallas kernels, weight_part(): pl.pallas_call(weight_kernel, grid_spec=pltpu.PrefetchScalarGridSpec(num_...  16.7 us
  transfers between devices with their start and end apart: 5, of which 5 were waited for; matrix products, arithmetic and copies ran while one was open for 1% of the time, Pallas kernels for 4%

commit v1 on v0

--- a/solution.py
+++ b/solution.py
@@ -74,10 +74,13 @@
         src, dst = ends(a, me, me)
         return pltpu.make_async_copy(src, dst, own.at[a])
 
-    for a in range(4):
+    def begin(a):
         for k in range(1, n):
             remote(a, mod(k), me).start()
         here(a).start()
+
+    for a in range(3):
+        begin(a)
 
     grads_ref[...] = jnp.zeros_like(grads_ref)
     lane = lax.broadcasted_iota(jnp.int32, (BLK, BLK), 1)
@@ -87,6 +90,7 @@
         here(a).wait()
         for k in range(1, n):
             remote(a, me, mod(k)).wait_recv()
+    begin(3)
 
     def prep(c, carry):
         keys = pl.ds(pl.multiple_of(c * BLK, BLK), BLK)
@@ -337,26 +341,39 @@
     for k in range(1, repeat):
         sent = lax.dynamic_index_in_dim(parts, rank ^ k, 0, keepdims=False)
         mine = mine + lax.ppermute(sent, "ctx", [(i, i ^ k) for i in range(n)])
-    gathered = lax.all_gather(mine.astype(bf16).T, "ctx", axis=0)
-    gathered = gathered.reshape(KV_HEADS, repeat, 2 * HD, kr)
-    mine_low = lax.dynamic_index_in_dim(gathered, me * kb // kr, 1, keepdims=False)
-    mine_low = lax.dynamic_slice_in_dim(mine_low, me * kb % kr, kb, 2)
-    grad_low = mine_low.transpose(2, 0, 1).reshape(kb, kv_width)
-
     cols = kv_width // dp
     per = 2 * HD // cols
-
-    def part(k, dtype):
+    half = cols // 2
+    pieces = mine.astype(bf16).T.reshape(per, 2, half, kr)
+    gathers = [
+        lax.all_gather(pieces[:, p].reshape(per * half, kr), "ctx", axis=0).reshape(
+            KV_HEADS, repeat, per * half, kr
+        )
+        for p in range(2)
+    ]
+
+    def own_rows(gathered):
+        x = lax.dynamic_index_in_dim(gathered, me * kb // kr, 1, keepdims=False)
+        x = lax.dynamic_slice_in_dim(x, me * kb % kr, kb, 2)
+        return x.reshape(KV_HEADS, per, half, kb)
+
+    grad_low = jnp.stack([own_rows(g) for g in gathers], axis=2).reshape(kv_width, kb).T
+
+    def part(k, p, dtype):
         t = (my_dp ^ k).astype(i32)
-        return weight_part(jnp.stack([t // per, t % per]), gathered, hid, cols, dtype)
-
-    sent = []
-    for k in sorted(range(1, dp), key=lambda k: (k != 2, k)):
-        sent.append(lax.ppermute(part(k, bf16), "dp", [(i, i ^ k) for i in range(dp)]))
-    weight = part(0, f32)
-
-    for s in sent:
-        weight = weight + s.astype(f32)
+        return weight_part(jnp.stack([t // per, t % per]), gathers[p], hid, half, dtype)
+
+    order = sorted(range(1, dp), key=lambda k: (k != 2, k))
+    sums = []
+    for p in range(2):
+        sent = [
+            lax.ppermute(part(k, p, bf16), "dp", [(i, i ^ k) for i in range(dp)]) for k in order
+        ]
+        weight = part(0, p, f32)
+        for other in sent:
+            weight = weight + other.astype(f32)
+        sums.append(weight)
+    weight = jnp.concatenate(sums, axis=0)
     return (attended[None], grad_query[None], grad_low[None], weight.T)
 
 

time: 356 us -> 379 us (1.065); the launches traced: 355 us -> 373 us
  Pallas kernels: 209 us -> 218 us
  waiting for transfers between devices: 96.7 us -> 103 us
  starting transfers between devices: 2.89 us -> 7.27 us
    all_gather x1 -> x2, waiting for transfers between devices: 47 us -> 66.4 us  [local(): lax.all_gather(pieces[:, p].reshape(per * half, kr), 'ctx', axis=0)]
    ppermute x3 -> x6, waiting for transfers between devices: 46.4 us -> 32.5 us  [local(): lax.ppermute(part(k, p, bf16), 'dp', [(i, i ^ k) for i in range(dp)])]
    pallas_call x4 -> x8, Pallas kernels: 16.7 us -> 25.8 us  [weight_part(): pl.pallas_call(weight_kernel, grid_spec=pltpu.PrefetchScalarGridSpec(num_...]
    dynamic_slice x4 -> x0, local copies, waits for them, and re-layouts: 5.73 us -> none  [the longest x2 2.56 us: local(): mine = lax.dynamic_index_in_dim(parts, rank, 0, keepdims=False)]
    another operation x1 -> x4, local copies, waits for them, and re-layouts: 0.12 us -> 4.31 us  [the longest x3 4.2 us: local(): jnp.stack([own_rows(g) for g in gathers], axis=2).reshape(kv_width, kb)]
    ppermute x3 -> x6, starting transfers between devices: 2.85 us -> 6.94 us  [local(): lax.ppermute(part(k, p, bf16), 'dp', [(i, i ^ k) for i in range(dp)])]
    unnamed x18 -> x26, local copies, waits for them, and re-layouts: 20 us -> 18.1 us
  transfers between devices with their start and end apart: 5 -> 9, of which waited for: 5 -> 6; matrix products, arithmetic and copies ran while one was open for 1% -> 2% of each run, Pallas kernels for 4% -> 5%
where the time goes in v1:
time: 379 us; the launch traced here: 373 us
  Pallas kernels  218 us (58%)
  waiting for transfers between devices  103 us (27%)
  local copies, waits for them, and re-layouts  25.3 us (7%)
  between operations  15 us (4%)
  starting transfers between devices  7.27 us (2%)
  other arithmetic  5 us (1%)
    pallas_call x1, Pallas kernels, attention(): pl.pallas_call(functools.partial(attention_kernel, heads, n), in_specs=[v...  192 us
    all_gather x2, waiting for transfers between devices, local(): lax.all_gather(pieces[:, p].reshape(per * half, kr), 'ctx', axis=0)  66.4 us
    ppermute x6, waiting for transfers between devices, local(): lax.ppermute(part(k, p, bf16), 'dp', [(i, i ^ k) for i in range(dp)])  32.5 us
    pallas_call x8, Pallas kernels, weight_part(): pl.pallas_call(weight_kernel, grid_spec=pltpu.PrefetchScalarGridSpec(num_...  25.8 us
    unnamed x26, local copies, waits for them, and re-layouts  18.1 us
  transfers between devices with their start and end apart: 9, of which 6 were waited for; matrix products, arithmetic and copies ran while one was open for 2% of the time, Pallas kernels for 5%

profile of v1, /device:TPU:17, one launch (start us, length us, event | category | flops | bytes accessed | tf_op | source)
XLA Modules:
  0.0 373.2 jit_solution(2989962744914899316)
XLA Ops:
  10.7 192.1 %attention.1 = (bf16[128,6144]{1,0:T(8,128)(2,1)}, bf16[128,6144]{1,0:T(8,128)(2,1)}, bf16[8,384,1536]{2,1,0:T(8,128)(2,1)}, f32[3072,256]{1,0:T(8,128)}) custom-call(s32[4,1,256]{2,1,0:T(1,128)S(1)} %add_maximum_fusion.low_ref, bf16[128,6144]{1,0:T(8,128)(2,1)} %bitcast.71, bf16[128,6144]{1,0:T(8,128)(2,1)} %bitcast.72, bf16[384,1024]{1,0:T(8,128)(2,1)S(1)} %bitcast.61, ...), custom_call_target="tpu_custom_call" | custom-call | flops 36238786560 | bytes 9437184 | tf_op jit(solution)/shard_map/attention/pallas_call | solution.py:235
  204.4 3.4 collective-permute-done
  207.8 1.6 fusion.1
  211.6 33.6 %all-gather.7.cloned.1.call-done = bf16[8,1,128,1536]{3,2,1,0:T(8,128)(2,1)} async-done(((bf16[1,1,128,1536]{3,2,1,0:T(8,128)(2,1)}), bf16[8,1,128,1536]{3,2,1,0:T(8,128)(2,1)}) %all-gather.7.cloned.1.call-update) | async-done | bytes 3145744 | tf_op jit(solution)/shard_map/all_gather | solution.py:349
  245.2 2.0 dynamic-slice_bitcast_fusion.1
  247.2 32.8 %all-gather.5.cloned.1.call-done = bf16[8,1,128,1536]{3,2,1,0:T(8,128)(2,1)} async-done(((bf16[1,1,128,1536]{3,2,1,0:T(8,128)(2,1)}), bf16[8,1,128,1536]{3,2,1,0:T(8,128)(2,1)}) %all-gather.5.cloned.1.call-update) | async-done | bytes 3145744 | tf_op jit(solution)/shard_map/all_gather | solution.py:349
  281.3 3.7 copy-done
  285.0 1.9 copy-done.2
  286.9 3.6 weight.15
  290.5 3.0 weight.11
  293.8 3.6 weight.14
  298.6 3.6 weight.13
  302.2 1.8 collective-permute-start.4
  304.1 3.0 weight.10
  308.8 2.3 copy.27
  312.8 3.7 copy-done.1
  316.5 3.0 weight.12
  319.5 3.0 weight.8
  322.5 3.0 weight.9
  325.5 1.9 collective-permute-start.1
  327.4 8.7 %collective-permute-done.4 = bf16[128,1536]{1,0:T(8,128)(2,1)} collective-permute-done((bf16[128,1536]{1,0:T(8,128)(2,1)}, bf16[128,1536]{1,0:T(8,128)(2,1)}, u32[]{:S(2)}, u32[]{:S(2)}) %collective-permute-start.4) | collective-permute-done | bytes 393248 | tf_op jit(solution)/shard_map/ppermute | solution.py:370
  337.5 17.3 %collective-permute-done.3 = bf16[128,1536]{1,0:T(8,128)(2,1)S(1)} collective-permute-done((bf16[128,1536]{1,0:T(8,128)(2,1)S(1)}, bf16[128,1536]{1,0:T(8,128)(2,1)S(1)}, u32[]{:S(2)}, u32[]{:S(2)}) %collective-permute-start.3) | collective-permute-done | bytes 393248 | tf_op jit(solution)/shard_map/ppermute | solution.py:370
  354.8 6.5 %collective-permute-done.1 = bf16[128,1536]{1,0:T(8,128)(2,1)S(1)} collective-permute-done((bf16[128,1536]{1,0:T(8,128)(2,1)S(1)}, bf16[128,1536]{1,0:T(8,128)(2,1)S(1)}, u32[]{:S(2)}, u32[]{:S(2)}) %collective-permute-start.1) | collective-permute-done | bytes 393248 | tf_op jit(solution)/shard_map/ppermute | solution.py:370
  361.6 1.6 copy.28
  (54 shorter events, 17.6 us)
Async XLA Ops:
  7.2 238.1 %all-gather.7.cloned.1.call-start = ((), (), s32[]{:S(2)}) async-start(), calls=%async_computation.1 | async-start | bytes 3538944 | tf_op jit(solution)/shard_map/all_gather | solution.py:349
  9.6 1.1 copy-start.7
  204.3 3.5 collective-permute-start
  210.6 69.4 %all-gather.5.cloned.1.call-start = ((), (), s32[]{:S(2)}) async-start(), calls=%async_computation | async-start | bytes 3538944 | tf_op jit(solution)/shard_map/all_gather | solution.py:349
  281.3 3.7 copy-start
  285.0 1.9 copy-start.2
  286.9 3.6 copy-start.4
  290.5 3.3 copy-start.3
  293.5 32.1 %collective-permute-start.6 = (bf16[128,1536]{1,0:T(8,128)(2,1)}, bf16[128,1536]{1,0:T(8,128)(2,1)}, u32[]{:S(2)}, u32[]{:S(2)}) collective-permute-start(bf16[128,1536]{1,0:T(8,128)(2,1)} %weight.15), channel_id=1, source_target_pairs={{0,24},{8,16},{16,8},{24,0},{1,25},{9,17},{17,9},{25,1},{2,26},{10... | collective-permute-start | bytes 1179656 | tf_op jit(solution)/shard_map/ppermute | solution.py:370
  297.4 6.6 %copy-start.10 = (bf16[4,1,1,128,384]{4,3,0,2,1:T(8,128)(2,1)S(1)}, bf16[4,1,1,128,384]{4,3,0,2,1:T(8,128)(2,1)}, u32[]{:S(2)}) copy-start(bf16[4,1,1,128,384]{4,3,0,2,1:T(8,128)(2,1)} %dynamic-slice_bitcast_fusion.1) | copy-start | bytes 1179652
  297.4 30.0 %collective-permute-start.5 = (bf16[128,1536]{1,0:T(8,128)(2,1)}, bf16[128,1536]{1,0:T(8,128)(2,1)}, u32[]{:S(2)}, u32[]{:S(2)}) collective-permute-start(bf16[128,1536]{1,0:T(8,128)(2,1)} %weight.14), channel_id=1, source_target_pairs={{0,8},{8,0},{16,24},{24,16},{1,9},{9,1},{17,25},{25,17},{2,10},{10... | collective-permute-start | bytes 1179656 | tf_op jit(solution)/shard_map/ppermute | solution.py:370
  302.2 34.0 %collective-permute-start.4 = (bf16[128,1536]{1,0:T(8,128)(2,1)}, bf16[128,1536]{1,0:T(8,128)(2,1)}, u32[]{:S(2)}, u32[]{:S(2)}) collective-permute-start(bf16[128,1536]{1,0:T(8,128)(2,1)} %weight.13), channel_id=1, source_target_pairs={{0,16},{8,24},{16,0},{24,8},{1,17},{9,25},{17,1},{25,9},{2,18},{10... | collective-permute-start | bytes 1179656 | tf_op jit(solution)/shard_map/ppermute | solution.py:370
  307.1 0.7 copy-start.6
  311.1 43.7 %collective-permute-start.3 = (bf16[128,1536]{1,0:T(8,128)(2,1)S(1)}, bf16[128,1536]{1,0:T(8,128)(2,1)S(1)}, u32[]{:S(2)}, u32[]{:S(2)}) collective-permute-start(bf16[128,1536]{1,0:T(8,128)(2,1)S(1)} %weight.11), channel_id=1, source_target_pairs={{0,24},{8,16},{16,8},{24,0},{1,25},{9,17},{17,9},{25,1},{2,26},{10... | collective-permute-start | bytes 1179656 | tf_op jit(solution)/shard_map/ppermute | solution.py:370
  311.4 43.4 %collective-permute-start.2 = (bf16[128,1536]{1,0:T(8,128)(2,1)}, bf16[128,1536]{1,0:T(8,128)(2,1)S(1)}, u32[]{:S(2)}, u32[]{:S(2)}) collective-permute-start(bf16[128,1536]{1,0:T(8,128)(2,1)} %copy-done.6), channel_id=1, source_target_pairs={{0,8},{8,0},{16,24},{24,16},{1,9},{9,1},{17,25},{25,17},{2,10},{10... | collective-permute-start | bytes 1179656 | tf_op jit(solution)/shard_map/ppermute | solution.py:370
  312.8 3.7 copy-start.1
  316.5 3.0 copy-start.5
  325.5 35.8 %collective-permute-start.1 = (bf16[128,1536]{1,0:T(8,128)(2,1)S(1)}, bf16[128,1536]{1,0:T(8,128)(2,1)S(1)}, u32[]{:S(2)}, u32[]{:S(2)}) collective-permute-start(bf16[128,1536]{1,0:T(8,128)(2,1)S(1)} %weight.9), channel_id=1, source_target_pairs={{0,16},{8,24},{16,0},{24,8},{1,17},{9,25},{17,1},{25,9},{2,18},{10... | collective-permute-start | bytes 1179656 | tf_op jit(solution)/shard_map/ppermute | solution.py:370
  361.6 1.6 copy-start.9
  363.2 2.0 copy-start.8
Sparse Core Ops, SparseCore 0:
  210.7 34.4 all-gather.6
  247.7 32.3 all-gather.4
